TPU v7x, 32 devices: a whole 2x2x4 slice. The times are simulated.
32 devices in a mesh: heads: 4 (over z), keys: 8 (over y, x, core).
Axes of the slice: x: 2, y: 2, z: 4, core: 2. Of those that a mesh axis runs over, the one named last changes fastest.
Arguments:
- queries: bfloat16 [2048, 4096], P('keys', 'heads')
- key_states: bfloat16 [65536, 4096], P('keys', 'heads')
- value_states: bfloat16 [65536, 4096], P('keys', 'heads'), may hold values from -6 to 6
- block_ids: int32 [32, 768], P('heads', 'keys'), may hold values from 0 to 1023, as said below
- block_counts: int32 [32, 8], P('heads', 'keys'), may hold values from 2 to 96, as said below
- out_weight: bfloat16 [4096, 4096], P('heads'), may hold values from -0.09375 to 0.09375
Outputs:
- projected: bfloat16 [2048, 4096], P('keys', 'heads')
Inputs may be any that keep to these rules, and one draw needn't show every extreme that they name: `block_ids`: entry h, r * 96 + j names query block b // 64 and tile b % 64 of key range r for head h; the first block_counts[h, r] entries of a head and key range are distinct, the rest are ignored; every query block is named by a counted entry of every head. `block_counts`: some head and key range has exactly 96 counted entries.
All inputs are finite; a program needn't handle non-finite values.
Results may differ from a plain program's by a relative error of at most 0.025.
Values may be sent and summed in bfloat16 or wider, within the bound.
A program may use at most 192 MiB of HBM per device.

v0:
```python
import jax
import jax.numpy as jnp
from jax import lax
from jax.sharding import PartitionSpec as P

BLOCK = 128


def local(queries, key_states, value_states, block_ids, block_counts, out_weight):
    heads_here, slot_total = block_ids.shape
    head_dim = key_states.shape[1] // heads_here
    key_rows = key_states.shape[0]
    tiles = key_rows // BLOCK
    every_query = lax.all_gather(queries, "keys", axis=0, tiled=True)
    query_count = every_query.shape[0]
    query_tiles = query_count // BLOCK
    query_flat = (
        every_query.reshape(query_tiles, BLOCK, heads_here, head_dim)
        .transpose(2, 0, 1, 3)
        .reshape(heads_here * query_tiles, BLOCK, head_dim)
    )
    key_flat = (
        key_states.reshape(tiles, BLOCK, heads_here, head_dim)
        .transpose(2, 0, 1, 3)
        .reshape(heads_here * tiles, BLOCK, head_dim)
    )
    value_flat = (
        value_states.reshape(tiles, BLOCK, heads_here, head_dim)
        .transpose(2, 0, 1, 3)
        .reshape(heads_here * tiles, BLOCK, head_dim)
    )
    group_count = 4
    group_width = slot_total // group_count

    def grouped(table):
        return table.reshape(heads_here, group_count, group_width).transpose(1, 0, 2)

    head_index = jnp.arange(heads_here, dtype=jnp.int32)[:, None]
    query_tile = grouped(block_ids // tiles)
    query_flat_id = grouped(block_ids // tiles + head_index * query_tiles)
    key_flat_id = grouped(block_ids % tiles + head_index * tiles)
    live_slot = grouped(jnp.arange(slot_total, dtype=jnp.int32)[None, :] < block_counts)
    tile_index = jnp.arange(query_tiles, dtype=jnp.int32)
    inverse_root = head_dim ** (-0.5)

    def group_scores(query_ids, key_ids):
        query_blocks = jnp.take(query_flat, query_ids, axis=0)
        key_blocks = jnp.take(key_flat, key_ids, axis=0)
        product = jnp.einsum(
            "hwid,hwjd->hwij", query_blocks, key_blocks, preferred_element_type=jnp.float32
        )
        return product * inverse_root

    def max_step(running_max, slot_group):
        query_part, query_ids, key_ids, live_part = slot_group
        scores = group_scores(query_ids, key_ids)
        block_best = jnp.where(live_part[..., None], scores.max(-1), -jnp.inf)
        one_hot = query_part[..., None] == tile_index
        candidate = jnp.where(one_hot[..., None], block_best[:, :, None, :], -jnp.inf).max(1)
        return (jnp.maximum(running_max, candidate), None)

    start_max = jnp.full((heads_here, query_tiles, BLOCK), -jnp.inf, jnp.float32)
    local_max, unused = lax.scan(
        max_step, start_max, (query_tile, query_flat_id, key_flat_id, live_slot)
    )
    row_max = lax.pmax(local_max.astype(jnp.bfloat16), "keys").astype(local_max.dtype)
    max_flat = row_max.reshape(heads_here * query_tiles, BLOCK)

    def sum_step(totals, slot_group):
        numerator, denominator = totals
        query_part, query_ids, key_ids, live_part = slot_group
        scores = group_scores(query_ids, key_ids)
        slot_max = jnp.take(max_flat, query_ids, axis=0)
        exp_terms = jnp.where(
            live_part[..., None, None], jnp.exp(scores - slot_max[..., None]), 0.0
        )
        value_blocks = jnp.take(value_flat, key_ids, axis=0)
        value_terms = jnp.einsum(
            "hwij,hwjd->hwid",
            exp_terms.astype(jnp.bfloat16),
            value_blocks,
            preferred_element_type=jnp.float32,
        )
        selector = (query_part[..., None] == tile_index).astype(jnp.float32)
        numerator = numerator + jnp.einsum(
            "hwq,hwid->hqid", selector, value_terms, precision=lax.Precision.HIGHEST
        )
        denominator = denominator + jnp.einsum(
            "hwq,hwi->hqi", selector, exp_terms.sum(-1), precision=lax.Precision.HIGHEST
        )
        return ((numerator, denominator), None)

    start_sums = (
        jnp.zeros((heads_here, query_tiles, BLOCK, head_dim), jnp.float32),
        jnp.zeros((heads_here, query_tiles, BLOCK), jnp.float32),
    )
    totals, unused = lax.scan(
        sum_step, start_sums, (query_tile, query_flat_id, key_flat_id, live_slot)
    )
    numerator = totals[0].reshape(heads_here, query_count, head_dim)
    denominator = totals[1].reshape(heads_here, query_count)
    row_sums, weight_sums = (
        lax.psum_scatter(
            numerator.astype(jnp.bfloat16), "keys", scatter_dimension=1, tiled=True
        ).astype(jnp.float32),
        lax.psum_scatter(
            denominator.astype(jnp.bfloat16), "keys", scatter_dimension=1, tiled=True
        ).astype(jnp.float32),
    )
    attention = (row_sums / weight_sums[..., None]).astype(jnp.bfloat16)
    own_rows = attention.shape[1]
    group_total = lax.axis_size("heads")
    column_span = out_weight.shape[1] // group_total
    flat_cols = attention.transpose(0, 2, 1).reshape(heads_here * head_dim, own_rows)
    copies = jnp.broadcast_to(flat_cols[None], (group_total,) + flat_cols.shape)
    pieces = out_weight.reshape(out_weight.shape[0], group_total, column_span).transpose(1, 0, 2)
    got_rows, got_weight = (
        lax.all_to_all(copies, "heads", split_axis=0, concat_axis=1, tiled=True),
        lax.all_to_all(pieces, "heads", split_axis=0, concat_axis=1, tiled=True),
    )
    projected = lax.dot_general(
        got_rows[0], got_weight[0], (((0,), (0,)), ((), ())), preferred_element_type=jnp.float32
    ).astype(jnp.bfloat16)
    return projected


def solution(mesh):
    in_specs = (
        P("keys", "heads"),
        P("keys", "heads"),
        P("keys", "heads"),
        P("heads", "keys"),
        P("heads", "keys"),
        P("heads", None),
    )
    out_specs = P("keys", "heads")
    return jax.shard_map(local, mesh=mesh, in_specs=in_specs, out_specs=out_specs, check_vma=False)
```

profile of v0, /device:TPU:0, one launch (start us, length us, event | category | flops | bytes accessed | tf_op | source)
XLA Modules:
  0.0 721.2 jit_solution(6030292572377382110)
XLA Ops:
  7.3 12.0 %copy.53 = bf16[1024,4096]{0,1:T(8,128)(2,1)} copy(bf16[1024,4096]{1,0:T(8,128)(2,1)} %param.19) | data formatting | bytes 16777216 | tf_op args[5]
  19.3 11.4 %copy.54 = bf16[1024,4,1024]{2,0,1:T(8,128)(2,1)} copy(bf16[1024,4,1024]{0,2,1:T(8,128)(2,1)} %bitcast.113) | data formatting | bytes 16777216 | tf_op jit(solution)/shard_map/reshape | solution.py:116
  37.5 11.7 %copy.58 = bf16[1024,8,8,128]{3,2,1,0:T(8,128)(2,1)S(1)} copy(bf16[1024,8,8,128]{3,1,2,0:T(8,128)(2,1)} %bitcast.115) | data formatting | bytes 33554432
  78.2 137.0 %while.24 = (s32[]{:T(128)}, bf16[8,16,128]{2,1,0:T(8,128)(2,1)S(1)}, s32[4,8,24]{2,1,0:T(8,128)S(1)}, pred[4,8,24]{2,1,0:T(8,128)(4,1)S(1)}, s32[4,8,24]{2,1,0:...) while((s32[]{:T(128)}, ...), condition=%wide.region_3.6_spmd.clone, body=%wide.region_0.5_spmd.clone.sunk | while | flops 818748672 | bytes 38103736 | solution.py:63
  78.5 13.8 %gather_fusion = bf16[192,128,128]{2,1,0:T(8,128)(2,1)} fusion(bf16[512,128,128]{2,1,0:T(8,128)(2,1)} %get-tuple-element.464, s32[1024]{0:T(1024)S(1)} %pad_clamp_fusion.10), kind=kCustom, calls=%fused_computation.1.clone.clone.1 | custom fusion | bytes 12583680 | tf_op jit(solution)/shard_map/while/body/eval_jaxpr/jit(_take)/gather | solution.py:48
  112.7 13.8 %gather_fusion = bf16[192,128,128]{2,1,0:T(8,128)(2,1)} fusion(bf16[512,128,128]{2,1,0:T(8,128)(2,1)} %get-tuple-element.464, s32[1024]{0:T(1024)S(1)} %pad_clamp_fusion.10), kind=kCustom, calls=%fused_computation.1.clone.clone.1 | custom fusion | bytes 12583680 | tf_op jit(solution)/shard_map/while/body/eval_jaxpr/jit(_take)/gather | solution.py:48
  146.9 13.8 %gather_fusion = bf16[192,128,128]{2,1,0:T(8,128)(2,1)} fusion(bf16[512,128,128]{2,1,0:T(8,128)(2,1)} %get-tuple-element.464, s32[1024]{0:T(1024)S(1)} %pad_clamp_fusion.10), kind=kCustom, calls=%fused_computation.1.clone.clone.1 | custom fusion | bytes 12583680 | tf_op jit(solution)/shard_map/while/body/eval_jaxpr/jit(_take)/gather | solution.py:48
  181.1 13.8 %gather_fusion = bf16[192,128,128]{2,1,0:T(8,128)(2,1)} fusion(bf16[512,128,128]{2,1,0:T(8,128)(2,1)} %get-tuple-element.464, s32[1024]{0:T(1024)S(1)} %pad_clamp_fusion.10), kind=kCustom, calls=%fused_computation.1.clone.clone.1 | custom fusion | bytes 12583680 | tf_op jit(solution)/shard_map/while/body/eval_jaxpr/jit(_take)/gather | solution.py:48
  215.2 25.2 %pmax.7 = bf16[128,128]{1,0:T(8,128)(2,1)S(1)} all-reduce(bf16[128,128]{1,0:T(8,128)(2,1)S(1)} %bitcast.123), channel_id=1, replica_groups=mesh['heads'=4,'keys'=8] {'keys'}, use_global_device_ids=true, to_apply=%region_4.7 | all-reduce | flops 16384 | bytes 65536 | tf_op jit(solution)/shard_map/pmax | solution.py:66
  240.5 326.4 %while.25 = (s32[]{:T(128)}, f32[8,16,128,128]{3,1,2,0:T(8,128)}, f32[8,16,128]{2,1,0:T(8,128)S(1)}, s32[4,8,24]{2,1,0:T(8,128)S(1)}, pred[4,8,24]{2,1,0:T(8,128...) while((s32[]{:T(128)}, f32[8,16,128,128]{3,1,2,0:T(8,128)}, ...), condition=%wide.region_7.10_spmd.clone, body=%wide.region_5.9_spmd.clone.sunk | while | flops 2258153216 | bytes 124706120 | solution.py:97
  242.3 13.8 %gather_fusion.3 = bf16[192,128,128]{2,1,0:T(8,128)(2,1)} fusion(bf16[512,128,128]{2,1,0:T(8,128)(2,1)} %get-tuple-element.501, s32[1024]{0:T(1024)S(1)} %pad_clamp_fusion.13), kind=kCustom, calls=%fused_computation.3.clone.clone.1 | custom fusion | bytes 12583680 | tf_op jit(solution)/shard_map/while/body/eval_jaxpr/jit(_take)/gather | solution.py:48
  266.3 10.4 %fusion.68 = (f32[8,24,128]{2,1,0:T(8,128)S(1)}, f32[8,24,128,128]{2,3,1,0:T(8,128)}) fusion(f32[8,24,128]{2,1,0:T(8,128)S(1)} %broadcast_select_fusion.5, pred[8,24]{1,0:T(8,128)(4,1)S(1)} %dynamic-slice_bitcast_fusion.10, bf16[8,24,128,128]{3,2,1,0:T(8,128)(2,1)} %bitcast.105, pred[8,24]{1,0:T(8,128)(4,1)S(1)} %get-tuple-element.433, ...), kind=kOutput, calls=%fused_computation.31.clone.1 | convolution fusion | flops 824156160 | bytes 25363008 | tf_op jit(solution)/shard_map/while/body/eval_jaxpr/hwid,hwjd->hwij/dot_general | solution.py:49
  276.8 13.9 %gather_fusion.5 = bf16[192,128,128]{2,1,0:T(8,128)(2,1)} fusion(bf16[512,128,128]{2,1,0:T(8,128)(2,1)} %get-tuple-element.503, s32[1024]{0:T(1024)S(1)} %pad_clamp_fusion.13), kind=kCustom, calls=%fused_computation.4.clone.clone.1 | custom fusion | bytes 12583680 | tf_op jit(solution)/shard_map/while/body/eval_jaxpr/jit(_take)/gather | solution.py:77
  290.6 11.0 %fusion.69 = f32[8,24,128,128]{3,2,1,0:T(8,128)} fusion(f32[8,24,128,128]{2,3,1,0:T(8,128)} %get-tuple-element.435, bf16[8,24,128,128]{3,2,1,0:T(8,128)(2,1)} %bitcast.103, f32[8,24,128]{2,1,0:T(8,128)S(1)} %broadcast_select_fusion.5, pred[8,24]{1,0:T(8,128)(4,1)S(1)} %get-tuple-element.433, pred[8,24]{1,0:T(8,128)(4,1)S(1)} %dynamic-slice_bitcast_fusion.10), kind=kOutput, calls=%fused_computation.34.clone.1 | convolution fusion | flops 821035008 | bytes 31555968 | tf_op jit(solution)/shard_map/while/body/eval_jaxpr/hwij,hwjd->hwid/dot_general | solution.py:78
  302.3 18.7 %select_add_fusion.2 = f32[8,16,128,128]{3,1,2,0:T(8,128)} fusion(f32[8,16,128,128]{3,1,2,0:T(8,128)} %get-tuple-element.481, pred[]{:T(512)S(6)} %compare.10, f32[8,24,128,128]{3,2,1,0:T(8,128)} %fusion.69, s32[8,24]{1,0:T(8,128)S(1)} %dynamic-slice_bitcast_fusion.11), kind=kOutput, calls=%fused_computation.33.clone.1 | convolution fusion | flops 608177152 | bytes 29360896 | tf_op jit(solution)/shard_map/while/body/eval_jaxpr/hwq,hwid->hqid/dot_general | solution.py:85
  322.9 13.8 %gather_fusion.3 = bf16[192,128,128]{2,1,0:T(8,128)(2,1)} fusion(bf16[512,128,128]{2,1,0:T(8,128)(2,1)} %get-tuple-element.501, s32[1024]{0:T(1024)S(1)} %pad_clamp_fusion.13), kind=kCustom, calls=%fused_computation.3.clone.clone.1 | custom fusion | bytes 12583680 | tf_op jit(solution)/shard_map/while/body/eval_jaxpr/jit(_take)/gather | solution.py:48
  346.9 10.4 %fusion.68 = (f32[8,24,128]{2,1,0:T(8,128)S(1)}, f32[8,24,128,128]{2,3,1,0:T(8,128)}) fusion(f32[8,24,128]{2,1,0:T(8,128)S(1)} %broadcast_select_fusion.5, pred[8,24]{1,0:T(8,128)(4,1)S(1)} %dynamic-slice_bitcast_fusion.10, bf16[8,24,128,128]{3,2,1,0:T(8,128)(2,1)} %bitcast.105, pred[8,24]{1,0:T(8,128)(4,1)S(1)} %get-tuple-element.433, ...), kind=kOutput, calls=%fused_computation.31.clone.1 | convolution fusion | flops 824156160 | bytes 25363008 | tf_op jit(solution)/shard_map/while/body/eval_jaxpr/hwid,hwjd->hwij/dot_general | solution.py:49
  357.3 13.9 %gather_fusion.5 = bf16[192,128,128]{2,1,0:T(8,128)(2,1)} fusion(bf16[512,128,128]{2,1,0:T(8,128)(2,1)} %get-tuple-element.503, s32[1024]{0:T(1024)S(1)} %pad_clamp_fusion.13), kind=kCustom, calls=%fused_computation.4.clone.clone.1 | custom fusion | bytes 12583680 | tf_op jit(solution)/shard_map/while/body/eval_jaxpr/jit(_take)/gather | solution.py:77
  371.2 11.0 %fusion.69 = f32[8,24,128,128]{3,2,1,0:T(8,128)} fusion(f32[8,24,128,128]{2,3,1,0:T(8,128)} %get-tuple-element.435, bf16[8,24,128,128]{3,2,1,0:T(8,128)(2,1)} %bitcast.103, f32[8,24,128]{2,1,0:T(8,128)S(1)} %broadcast_select_fusion.5, pred[8,24]{1,0:T(8,128)(4,1)S(1)} %get-tuple-element.433, pred[8,24]{1,0:T(8,128)(4,1)S(1)} %dynamic-slice_bitcast_fusion.10), kind=kOutput, calls=%fused_computation.34.clone.1 | convolution fusion | flops 821035008 | bytes 31555968 | tf_op jit(solution)/shard_map/while/body/eval_jaxpr/hwij,hwjd->hwid/dot_general | solution.py:78
  382.9 19.9 %select_add_fusion.2 = f32[8,16,128,128]{3,1,2,0:T(8,128)} fusion(f32[8,16,128,128]{3,1,2,0:T(8,128)} %get-tuple-element.481, pred[]{:T(512)S(6)} %compare.10, f32[8,24,128,128]{3,2,1,0:T(8,128)} %fusion.69, s32[8,24]{1,0:T(8,128)S(1)} %dynamic-slice_bitcast_fusion.11), kind=kOutput, calls=%fused_computation.33.clone.1 | convolution fusion | flops 608177152 | bytes 29360896 | tf_op jit(solution)/shard_map/while/body/eval_jaxpr/hwq,hwid->hqid/dot_general | solution.py:85
  404.7 13.8 %gather_fusion.3 = bf16[192,128,128]{2,1,0:T(8,128)(2,1)} fusion(bf16[512,128,128]{2,1,0:T(8,128)(2,1)} %get-tuple-element.501, s32[1024]{0:T(1024)S(1)} %pad_clamp_fusion.13), kind=kCustom, calls=%fused_computation.3.clone.clone.1 | custom fusion | bytes 12583680 | tf_op jit(solution)/shard_map/while/body/eval_jaxpr/jit(_take)/gather | solution.py:48
  428.7 10.4 %fusion.68 = (f32[8,24,128]{2,1,0:T(8,128)S(1)}, f32[8,24,128,128]{2,3,1,0:T(8,128)}) fusion(f32[8,24,128]{2,1,0:T(8,128)S(1)} %broadcast_select_fusion.5, pred[8,24]{1,0:T(8,128)(4,1)S(1)} %dynamic-slice_bitcast_fusion.10, bf16[8,24,128,128]{3,2,1,0:T(8,128)(2,1)} %bitcast.105, pred[8,24]{1,0:T(8,128)(4,1)S(1)} %get-tuple-element.433, ...), kind=kOutput, calls=%fused_computation.31.clone.1 | convolution fusion | flops 824156160 | bytes 25363008 | tf_op jit(solution)/shard_map/while/body/eval_jaxpr/hwid,hwjd->hwij/dot_general | solution.py:49
  439.1 13.9 %gather_fusion.5 = bf16[192,128,128]{2,1,0:T(8,128)(2,1)} fusion(bf16[512,128,128]{2,1,0:T(8,128)(2,1)} %get-tuple-element.503, s32[1024]{0:T(1024)S(1)} %pad_clamp_fusion.13), kind=kCustom, calls=%fused_computation.4.clone.clone.1 | custom fusion | bytes 12583680 | tf_op jit(solution)/shard_map/while/body/eval_jaxpr/jit(_take)/gather | solution.py:77
  453.0 11.0 %fusion.69 = f32[8,24,128,128]{3,2,1,0:T(8,128)} fusion(f32[8,24,128,128]{2,3,1,0:T(8,128)} %get-tuple-element.435, bf16[8,24,128,128]{3,2,1,0:T(8,128)(2,1)} %bitcast.103, f32[8,24,128]{2,1,0:T(8,128)S(1)} %broadcast_select_fusion.5, pred[8,24]{1,0:T(8,128)(4,1)S(1)} %get-tuple-element.433, pred[8,24]{1,0:T(8,128)(4,1)S(1)} %dynamic-slice_bitcast_fusion.10), kind=kOutput, calls=%fused_computation.34.clone.1 | convolution fusion | flops 821035008 | bytes 31555968 | tf_op jit(solution)/shard_map/while/body/eval_jaxpr/hwij,hwjd->hwid/dot_general | solution.py:78
  464.7 19.9 %select_add_fusion.2 = f32[8,16,128,128]{3,1,2,0:T(8,128)} fusion(f32[8,16,128,128]{3,1,2,0:T(8,128)} %get-tuple-element.481, pred[]{:T(512)S(6)} %compare.10, f32[8,24,128,128]{3,2,1,0:T(8,128)} %fusion.69, s32[8,24]{1,0:T(8,128)S(1)} %dynamic-slice_bitcast_fusion.11), kind=kOutput, calls=%fused_computation.33.clone.1 | convolution fusion | flops 608177152 | bytes 29360896 | tf_op jit(solution)/shard_map/while/body/eval_jaxpr/hwq,hwid->hqid/dot_general | solution.py:85
  486.5 13.8 %gather_fusion.3 = bf16[192,128,128]{2,1,0:T(8,128)(2,1)} fusion(bf16[512,128,128]{2,1,0:T(8,128)(2,1)} %get-tuple-element.501, s32[1024]{0:T(1024)S(1)} %pad_clamp_fusion.13), kind=kCustom, calls=%fused_computation.3.clone.clone.1 | custom fusion | bytes 12583680 | tf_op jit(solution)/shard_map/while/body/eval_jaxpr/jit(_take)/gather | solution.py:48
  520.9 13.9 %gather_fusion.5 = bf16[192,128,128]{2,1,0:T(8,128)(2,1)} fusion(bf16[512,128,128]{2,1,0:T(8,128)(2,1)} %get-tuple-element.503, s32[1024]{0:T(1024)S(1)} %pad_clamp_fusion.13), kind=kCustom, calls=%fused_computation.4.clone.clone.1 | custom fusion | bytes 12583680 | tf_op jit(solution)/shard_map/while/body/eval_jaxpr/jit(_take)/gather | solution.py:77
  534.8 11.0 %fusion.69 = f32[8,24,128,128]{3,2,1,0:T(8,128)} fusion(f32[8,24,128,128]{2,3,1,0:T(8,128)} %get-tuple-element.435, bf16[8,24,128,128]{3,2,1,0:T(8,128)(2,1)} %bitcast.103, f32[8,24,128]{2,1,0:T(8,128)S(1)} %broadcast_select_fusion.5, pred[8,24]{1,0:T(8,128)(4,1)S(1)} %get-tuple-element.433, pred[8,24]{1,0:T(8,128)(4,1)S(1)} %dynamic-slice_bitcast_fusion.10), kind=kOutput, calls=%fused_computation.34.clone.1 | convolution fusion | flops 821035008 | bytes 31555968 | tf_op jit(solution)/shard_map/while/body/eval_jaxpr/hwij,hwjd->hwid/dot_general | solution.py:78
  546.5 19.9 %select_add_fusion.2 = f32[8,16,128,128]{3,1,2,0:T(8,128)} fusion(f32[8,16,128,128]{3,1,2,0:T(8,128)} %get-tuple-element.481, pred[]{:T(512)S(6)} %compare.10, f32[8,24,128,128]{3,2,1,0:T(8,128)} %fusion.69, s32[8,24]{1,0:T(8,128)S(1)} %dynamic-slice_bitcast_fusion.11), kind=kOutput, calls=%fused_computation.33.clone.1 | convolution fusion | flops 608177152 | bytes 29360896 | tf_op jit(solution)/shard_map/while/body/eval_jaxpr/hwq,hwid->hqid/dot_general | solution.py:85
  575.7 22.2 %reduce-scatter.5.cloned.1.call-done = bf16[8,256]{1,0:T(8,128)(2,1)} async-done(((bf16[8,2048]{1,0:T(8,128)(2,1)}), bf16[8,256]{1,0:T(8,128)(2,1)}) %reduce-scatter.5.cloned.1.call-update) | async-done | bytes 4112 | tf_op jit(solution)/shard_map/reduce_scatter | solution.py:106
  598.6 54.4 %reduce-scatter.3.cloned.1.call-done = bf16[8,256,128]{2,1,0:T(8,128)(2,1)} async-done(((bf16[8,2048,128]{2,1,0:T(8,128)(2,1)}), bf16[8,256,128]{2,1,0:T(8,128)(2,1)}) %reduce-scatter.3.cloned.1.call-update) | async-done | bytes 524304 | tf_op jit(solution)/shard_map/reduce_scatter | solution.py:103
  655.1 52.6 %all_to_all.8 = bf16[4,1024,256]{1,2,0:T(8,128)(2,1)S(1)} all-to-all(bf16[4,1024,256]{1,2,0:T(8,128)(2,1)S(1)} %broadcast_in_dim.108), channel_id=1, replica_groups=mesh['heads'=4,'keys'=8] {'heads'}, dimensions={0} | all-to-all | bytes 4194304 | tf_op jit(solution)/shard_map/all_to_all | solution.py:118
  (175 shorter events, 197.2 us)
Async XLA Ops:
  6.5 65.3 %all-gather.2.cloned.1.call-start = ((), (), s32[]{:S(2)}) async-start(), calls=%async_computation.4 | async-start | bytes 4718592 | tf_op jit(solution)/shard_map/all_gather | solution.py:14
  30.7 6.5 copy-start.2
  30.7 624.1 %all-to-all-start.1 = ((bf16[4,1024,1024]{2,1,0:T(8,128)(2,1)}), bf16[4,1024,1024]{2,1,0:T(8,128)(2,1)}, u32[]{:S(2)}, u32[]{:S(2)}) async-start(bf16[4,1024,1024]{2,1,0:T(8,128)(2,1)} %bitcast.112), calls=%async_computation.3 | async-start | bytes 16777216 | tf_op jit(solution)/shard_map/all_to_all | solution.py:119
  37.2 560.7 %reduce-scatter.5.cloned.1.call-start = ((), (), s32[]{:S(2)}) async-start(), calls=%async_computation.6 | async-start | bytes 36864 | tf_op jit(solution)/shard_map/reduce_scatter | solution.py:106
  37.5 21.1 %slice-start = ((s8[16777216]{0:T(1024)(128)(4,1)}), s8[4194304]{0:T(1024)(128)(4,1)S(1)}, s32[]{:S(2)}) async-start(s8[16777216]{0:T(1024)(128)(4,1)} %bitcast.116), calls=%async_computation.7 | async-start | bytes 8388608
  37.5 21.1 %slice-start.1 = ((s8[16777216]{0:T(1024)(128)(4,1)}), s8[4194304]{0:T(1024)(128)(4,1)S(1)}, s32[]{:S(2)}) async-start(s8[16777216]{0:T(1024)(128)(4,1)} %bitcast.116), calls=%async_computation.8 | async-start | bytes 8388608
  49.2 9.4 %slice-start.2 = ((s8[16777216]{0:T(1024)(128)(4,1)}), s8[4194304]{0:T(1024)(128)(4,1)S(1)}, s32[]{:S(2)}) async-start(s8[16777216]{0:T(1024)(128)(4,1)} %bitcast.116), calls=%async_computation.9 | async-start | bytes 8388608
  49.3 9.4 %slice-start.3 = ((s8[16777216]{0:T(1024)(128)(4,1)}), s8[4194304]{0:T(1024)(128)(4,1)S(1)}, s32[]{:S(2)}) async-start(s8[16777216]{0:T(1024)(128)(4,1)} %bitcast.116), calls=%async_computation.10 | async-start | bytes 8388608
  62.5 9.3 %copy-start.3 = (s32[8,1]{0,1:T(1,128)S(1)}, s32[8,1]{0,1:T(1,128)}, u32[]{:S(2)}) copy-start(s32[8,1]{0,1:T(1,128)} %param.18) | copy-start | bytes 100
  240.7 0.6 copy-start
  302.3 18.9 %copy-start.1 = (s32[4,8,24]{2,1,0:T(8,128)S(1)}, s32[4,8,24]{2,1,0:T(8,128)}, u32[]{:S(2)}) copy-start(s32[4,8,24]{2,1,0:T(8,128)} %copy-done) | copy-start | bytes 9220 | tf_op jit(solution)/shard_map/while
  321.3 0.6 copy-start
  382.9 20.1 %copy-start.1 = (s32[4,8,24]{2,1,0:T(8,128)S(1)}, s32[4,8,24]{2,1,0:T(8,128)}, u32[]{:S(2)}) copy-start(s32[4,8,24]{2,1,0:T(8,128)} %copy-done) | copy-start | bytes 9220 | tf_op jit(solution)/shard_map/while
  403.1 0.6 copy-start
  464.7 20.1 %copy-start.1 = (s32[4,8,24]{2,1,0:T(8,128)S(1)}, s32[4,8,24]{2,1,0:T(8,128)}, u32[]{:S(2)}) copy-start(s32[4,8,24]{2,1,0:T(8,128)} %copy-done) | copy-start | bytes 9220 | tf_op jit(solution)/shard_map/while
  484.9 0.6 copy-start
  546.5 20.1 %copy-start.1 = (s32[4,8,24]{2,1,0:T(8,128)S(1)}, s32[4,8,24]{2,1,0:T(8,128)}, u32[]{:S(2)}) copy-start(s32[4,8,24]{2,1,0:T(8,128)} %copy-done) | copy-start | bytes 9220 | tf_op jit(solution)/shard_map/while
  567.6 85.4 %reduce-scatter.3.cloned.1.call-start = ((), (), s32[]{:S(2)}) async-start(), calls=%async_computation.5 | async-start | bytes 4718592 | tf_op jit(solution)/shard_map/reduce_scatter | solution.py:103
Sparse Core Ops, SparseCore 0:
  9.2 39.4 all-gather.1
  567.7 30.1 reduce-scatter.4
  601.6 51.3 reduce-scatter.2
where the time goes:
time: 734 us; the launch traced here: 721 us
  local copies, waits for them, and re-layouts  330 us (45%)
  matrix products  208 us (28%)
  blocking collectives  77.8 us (11%)
  waiting for transfers between devices  77.4 us (11%)
  between operations  13.7 us (2%)
    gather x8, local copies, waits for them, and re-layouts, group_scores(): key_blocks = jnp.take(key_flat, key_ids, axis=0)  110 us
    gather x8, local copies, waits for them, and re-layouts, group_scores(): query_blocks = jnp.take(query_flat, query_ids, axis=0)  81.3 us
    dot_general x4, matrix products, sum_step(): jnp.einsum('hwq,hwid->hqid', selector, value_terms, precision=lax.Precisi...  78.6 us
    dot_general x8, matrix products, group_scores(): jnp.einsum('hwid,hwjd->hwij', query_blocks, key_blocks, preferred_element...  78.5 us
    gather x4, local copies, waits for them, and re-layouts, sum_step(): value_blocks = jnp.take(value_flat, key_ids, axis=0)  55.4 us
    reduce_scatter x1, waiting for transfers between devices, local(): lax.psum_scatter(numerator.astype(jnp.bfloat16), 'keys', scatter_dimensio...  54.4 us
    all_to_all x1, blocking collectives, local(): lax.all_to_all(copies, 'heads', split_axis=0, concat_axis=1, tiled=True)  52.6 us
    dot_general x4, matrix products, sum_step(): jnp.einsum('hwij,hwjd->hwid', exp_terms.astype(jnp.bfloat16), value_block...  44.1 us
  transfers between devices with their start and end apart: 4, of which 2 were waited for; matrix products, arithmetic and copies ran while one was open for 74% of the time, Pallas kernels for 0%

commit v1 on v0

v1 whole, which is shorter than its diff:
```python
import functools
import math

import jax
import jax.numpy as jnp
from jax import lax
from jax.experimental import pallas as pl
from jax.experimental.pallas import tpu as pltpu
from jax.sharding import PartitionSpec as P

BLOCK = 128
UNROLL = 4


def attend(unroll, tiles, coef, ids, counts, qt_ref, k_ref, v_ref, num_ref, ml_ref, acc, mx, den):
    head = pl.program_id(0)
    query_tiles = qt_ref.shape[0]
    count = counts[head]
    acc[...] = jnp.zeros_like(acc)
    den[...] = jnp.zeros_like(den)
    mx[...] = jnp.full_like(mx, -jnp.inf)

    @pl.loop(0, (count + unroll - 1) // unroll)
    def _(step):
        done = []
        for u in range(unroll):
            slot = step * unroll + u
            live = slot < count
            entry = ids[head, jnp.where(live, slot, 0)]
            query = entry // tiles
            row = pl.multiple_of((entry % tiles) * BLOCK, BLOCK)
            scores = jnp.dot(
                k_ref[pl.ds(row, BLOCK), :], qt_ref[query, 0], preferred_element_type=jnp.float32
            )
            best = scores.max(0, keepdims=True)
            terms = jnp.exp2((scores - best) * coef)
            total = terms.sum(0, keepdims=True)
            values = lax.dot_general(
                v_ref[pl.ds(row, BLOCK), :],
                terms.astype(jnp.bfloat16),
                (((0,), (0,)), ((), ())),
                preferred_element_type=jnp.float32,
            )
            done.append((jnp.where(live, query, query_tiles), best, total, values))
        for query, best, total, values in done:
            old = mx[query]
            new = jnp.maximum(old, best)
            keep = jnp.exp2((old - new) * coef)
            take = jnp.exp2((best - new) * coef)
            mx[query] = new
            den[query] = den[query] * keep + total * take
            acc[query] = acc[query] * keep + values * take

    num_ref[...] = acc[:query_tiles].astype(num_ref.dtype)[:, None]
    ml_ref[:, 0, 0:1] = mx[:query_tiles]
    ml_ref[:, 0, 1:2] = den[:query_tiles]


def partials(query_cols, key_states, value_states, ids, counts, coef):
    query_tiles, heads_here, head_dim, _ = query_cols.shape
    key_rows = key_states.shape[0]
    tiles = key_rows // BLOCK
    return pl.pallas_call(
        functools.partial(attend, UNROLL, tiles, coef),
        grid_spec=pltpu.PrefetchScalarGridSpec(
            num_scalar_prefetch=2,
            grid=(heads_here,),
            in_specs=[
                pl.BlockSpec((query_tiles, 1, head_dim, BLOCK), lambda h, *_: (0, h, 0, 0)),
                pl.BlockSpec((key_rows, head_dim), lambda h, *_: (0, h)),
                pl.BlockSpec((key_rows, head_dim), lambda h, *_: (0, h)),
            ],
            out_specs=[
                pl.BlockSpec((query_tiles, 1, head_dim, BLOCK), lambda h, *_: (0, h, 0, 0)),
                pl.BlockSpec((query_tiles, 1, 2, BLOCK), lambda h, *_: (0, h, 0, 0)),
            ],
            scratch_shapes=[
                pltpu.VMEM((query_tiles + 1, head_dim, BLOCK), jnp.float32),
                pltpu.VMEM((query_tiles + 1, 1, BLOCK), jnp.float32),
                pltpu.VMEM((query_tiles + 1, 1, BLOCK), jnp.float32),
            ],
        ),
        out_shape=[
            jax.ShapeDtypeStruct((query_tiles, heads_here, head_dim, BLOCK), jnp.bfloat16),
            jax.ShapeDtypeStruct((query_tiles, heads_here, 2, BLOCK), jnp.float32),
        ],
        compiler_params=pltpu.CompilerParams(vmem_limit_bytes=48 << 20),
        name="block_attention",
    )(ids, counts, query_cols, key_states, value_states)


def local(queries, key_states, value_states, block_ids, block_counts, out_weight):
    heads_here, _ = block_ids.shape
    head_dim = key_states.shape[1] // heads_here
    own_rows = queries.shape[0]
    own_tiles = own_rows // BLOCK
    key_groups = lax.axis_size("keys")
    coef = head_dim ** (-0.5) * math.log2(math.e)
    own_cols = queries.reshape(own_tiles, BLOCK, heads_here, head_dim).transpose(0, 2, 3, 1)
    query_cols = lax.all_gather(own_cols, "keys", axis=0, tiled=True)
    num, ml = partials(
        query_cols, key_states, value_states, block_ids, block_counts[:, 0], coef
    )
    num = lax.all_to_all(num, "keys", split_axis=0, concat_axis=0, tiled=True)
    ml = lax.all_to_all(ml, "keys", split_axis=0, concat_axis=0, tiled=True)
    num = num.reshape(key_groups, own_tiles, heads_here, head_dim, BLOCK)
    ml = ml.reshape(key_groups, own_tiles, heads_here, 2, BLOCK)
    best = ml[:, :, :, 0]
    factor = jnp.exp2((best - best.max(0)) * coef)
    weight_sum = (ml[:, :, :, 1] * factor).sum(0)
    row_sum = (num.astype(jnp.float32) * factor[:, :, :, None]).sum(0)
    attention = (row_sum / weight_sum[:, :, None]).astype(jnp.bfloat16)
    flat = attention.transpose(0, 3, 1, 2).reshape(own_rows, heads_here * head_dim)
    part = jnp.dot(flat, out_weight, preferred_element_type=jnp.float32).astype(jnp.bfloat16)
    return lax.psum_scatter(part, "heads", scatter_dimension=1, tiled=True)


def solution(mesh):
    in_specs = (
        P("keys", "heads"),
        P("keys", "heads"),
        P("keys", "heads"),
        P("heads", "keys"),
        P("heads", "keys"),
        P("heads", None),
    )
    out_specs = P("keys", "heads")
    return jax.shard_map(local, mesh=mesh, in_specs=in_specs, out_specs=out_specs, check_vma=False)
```

time: 734 us -> 218 us (0.30); the launches traced: 721 us -> 220 us
  local copies, waits for them, and re-layouts: 330 us -> 5.99 us
  matrix products: 208 us -> 7.06 us
  blocking collectives: 77.8 us -> 12.2 us
  waiting for transfers between devices: 77.4 us -> 136 us
  Pallas kernels: 0 us -> 37.2 us
    gather x24 -> x0, local copies, waits for them, and re-layouts: 250 us -> none  [the longest x8 110 us: group_scores(): key_blocks = jnp.take(key_flat, key_ids, axis=0)]
    dot_general x21 -> x1, matrix products: 208 us -> 7.06 us  [local(): jnp.dot(flat, out_weight, preferred_element_type=jnp.float32)]
    all_to_all x1, waiting for transfers between devices: 0.01 us -> 48.9 us  [local(): num = lax.all_to_all(num, 'keys', split_axis=0, concat_axis=0, tiled=True)]
    all_to_all x1, blocking collectives: 52.6 us -> 12.2 us  [local(): ml = lax.all_to_all(ml, 'keys', split_axis=0, concat_axis=0, tiled=True)]
    all_gather x1, waiting for transfers between devices: 0.01 us -> 39.8 us  [local(): query_cols = lax.all_gather(own_cols, 'keys', axis=0, tiled=True)]
    pallas_call x0 -> x1, Pallas kernels: none -> 37.2 us  [partials(): pl.pallas_call(functools.partial(attend, UNROLL, tiles, coef), grid_spec=...]
    reshape x7 -> x0, local copies, waits for them, and re-layouts: 33.4 us -> none  [the longest x1 11.4 us: local(): out_weight.reshape(out_weight.shape[0], group_total, column_span)]
    reduce_scatter x2 -> x1, waiting for transfers between devices: 76.6 us -> 47.1 us  [local(): return lax.psum_scatter(part, 'heads', scatter_dimension=1, tiled=True)]
  transfers between devices with their start and end apart: 4 -> 3, of which waited for: 2 -> 3; matrix products, arithmetic and copies ran while one was open for 74% -> 0% of each run, Pallas kernels for 0% -> 0%
where the time goes in v1:
time: 218 us; the launch traced here: 220 us
  waiting for transfers between devices  136 us (62%)
  Pallas kernels  37.2 us (17%)
  between operations  13.5 us (6%)
  blocking collectives  12.2 us (6%)
  matrix products  7.06 us (3%)
  local copies, waits for them, and re-layouts  5.99 us (3%)
  starting transfers between devices  4.58 us (2%)
  other arithmetic  3.6 us (2%)
    all_to_all x1, waiting for transfers between devices, local(): num = lax.all_to_all(num, 'keys', split_axis=0, concat_axis=0, tiled=True)  48.9 us
    reduce_scatter x1, waiting for transfers between devices, local(): return lax.psum_scatter(part, 'heads', scatter_dimension=1, tiled=True)  47.1 us
    all_gather x1, waiting for transfers between devices, local(): query_cols = lax.all_gather(own_cols, 'keys', axis=0, tiled=True)  39.8 us
    pallas_call x1, Pallas kernels, partials(): pl.pallas_call(functools.partial(attend, UNROLL, tiles, coef), grid_spec=...  37.2 us
    all_to_all x1, blocking collectives, local(): ml = lax.all_to_all(ml, 'keys', split_axis=0, concat_axis=0, tiled=True)  12.2 us
    dot_general x1, matrix products, local(): jnp.dot(flat, out_weight, preferred_element_type=jnp.float32)  7.06 us
    all_to_all x1, starting transfers between devices, local(): num = lax.all_to_all(num, 'keys', split_axis=0, concat_axis=0, tiled=True)  4.53 us
    unnamed x7, local copies, waits for them, and re-layouts  4.43 us
  transfers between devices with their start and end apart: 3, of which 3 were waited for; matrix products, arithmetic and copies ran while one was open for 0% of the time, Pallas kernels for 0%

profile of v1, /device:TPU:0, one launch (start us, length us, event | category | flops | bytes accessed | tf_op | source)
XLA Modules:
  0.0 220.0 jit_solution(701947908114432197)
XLA Ops:
  6.5 0.0 all-gather.2.cloned.1.call-start
  6.5 1.1 copy.16
  7.7 1.1 copy.10
  8.8 0.0 all-gather.2.cloned.1.call-update
  8.9 39.8 %all-gather.2.cloned.1.call-done.qt_ref = bf16[16,8,128,128]{3,2,1,0:T(8,128)(2,1)} async-done(((bf16[2,8,128,128]{3,2,1,0:T(8,128)(2,1)}), bf16[16,8,128,128]{3,2,1,0:T(8,128)(2,1)}) %all-gather.2.cloned.1.call-update) | async-done | bytes 4194320 | tf_op jit(solution)/shard_map/all_gather | solution.py:100
  48.7 0.0 copy-start.1
  48.7 0.7 copy-done.1
  49.4 0.0 copy-start.2
  49.4 0.7 copy-done.2
  50.0 37.2 %block_attention.1 = (bf16[16,8,128,128]{3,2,1,0:T(8,128)(2,1)S(1)}, f32[16,8,2,128]{3,2,1,0:T(2,128)S(1)}) custom-call(s32[8,96]{1,0:T(8,128)S(1)} %copy-done.1, s32[8]{0:T(128)S(1)} %bitcast.30, bf16[16,8,128,128]{3,2,1,0:T(8,128)(2,1)} %all-gather.2.cloned.1.call-done.qt_ref, bf16[8192,1024]{1,0:T(8,128)(2,1)} %k_ref.1, bf16[8192,1024]{1,0:T(8,128)(2,1)} %v_ref.1), custom_call_target="tpu_custom_call" | custom-call | tf_op jit(solution)/shard_map/block_attention/pallas_call | solution.py:63
  87.2 0.0 copy-start
  87.2 2.0 copy-done
  89.2 12.2 %all_to_all.10 = f32[16,8,2,128]{3,2,1,0:T(2,128)S(1)} all-to-all(f32[16,8,2,128]{3,2,1,0:T(2,128)S(1)} %get-tuple-element.8), channel_id=1, replica_groups=mesh['heads'=4,'keys'=8] {'keys'}, dimensions={0} | all-to-all | bytes 262144 | tf_op jit(solution)/shard_map/all_to_all | solution.py:105
  101.4 4.5 %all-to-all-start = ((bf16[16,8,128,128]{3,2,1,0:T(8,128)(2,1)}), bf16[16,8,128,128]{3,2,1,0:T(8,128)(2,1)}, u32[]{:S(2)}, u32[]{:S(2)}) async-start(bf16[16,8,128,128]{3,2,1,0:T(8,128)(2,1)} %copy-done), calls=%async_computation | async-start | bytes 8388608 | tf_op jit(solution)/shard_map/all_to_all | solution.py:104
  105.9 0.0 reduce-scatter.2.cloned.1.call-start
  106.0 0.1 fusion.4
  106.2 48.9 %all-to-all-done = bf16[16,8,128,128]{3,2,1,0:T(8,128)(2,1)} async-done(((bf16[16,8,128,128]{3,2,1,0:T(8,128)(2,1)}), bf16[16,8,128,128]{3,2,1,0:T(8,128)(2,1)}, u32[]{:S(2)}, u32[]{:S(2)}) %all-to-all-start) | async-done | bytes 4194336 | tf_op jit(solution)/shard_map/all_to_all | solution.py:104
  155.1 3.4 %fusion = f32[2,8,128,128]{3,2,1,0:T(8,128)S(1)} fusion(bf16[8,2,8,128,128]{4,3,2,1,0:T(8,128)(2,1)} %bitcast.9, f32[8,2,8,128]{3,2,1,0:T(8,128)S(1)} %exponential_bitcast_fusion), kind=kLoop, calls=%fused_computation.1 | loop fusion | flops 6029312 | bytes 5308416 | tf_op jit(solution)/shard_map/reduce_sum | solution.py:111
  158.5 0.1 fusion.1
  158.6 0.3 copy.13
  158.9 7.1 %convolution_convert_fusion = bf16[256,4096]{1,0:T(8,128)(2,1)} fusion(bf16[1024,4096]{1,0:T(8,128)(2,1)} %param.11, bf16[32,8,8,128]{3,2,1,0:T(8,128)(2,1)S(1)} %bitcast.36), kind=kOutput, calls=%fused_computation.2 | convolution fusion | flops 2148532224 | bytes 11010048 | tf_op jit(solution)/shard_map/dot_general | solution.py:114
  166.0 0.0 reduce-scatter.2.cloned.1.call-update
  166.0 47.1 %reduce-scatter.2.cloned.1.call-done = bf16[256,1024]{1,0:T(8,128)(2,1)} async-done(((bf16[256,4096]{1,0:T(8,128)(2,1)}), bf16[256,1024]{1,0:T(8,128)(2,1)}) %reduce-scatter.2.cloned.1.call-update) | async-done | bytes 524304 | tf_op jit(solution)/shard_map/reduce_scatter | solution.py:115
  (4 shorter events, 0.1 us)
Async XLA Ops:
  6.5 42.2 %all-gather.2.cloned.1.call-start = ((), (), s32[]{:S(2)}) async-start(), calls=%async_computation.3 | async-start | bytes 4718592 | tf_op jit(solution)/shard_map/all_gather | solution.py:100
  48.7 0.7 copy-start.1
  49.4 0.7 copy-start.2
  87.2 2.0 copy-start
  101.4 53.7 %all-to-all-start = ((bf16[16,8,128,128]{3,2,1,0:T(8,128)(2,1)}), bf16[16,8,128,128]{3,2,1,0:T(8,128)(2,1)}, u32[]{:S(2)}, u32[]{:S(2)}) async-start(bf16[16,8,128,128]{3,2,1,0:T(8,128)(2,1)} %copy-done), calls=%async_computation | async-start | bytes 8388608 | tf_op jit(solution)/shard_map/all_to_all | solution.py:104
  105.9 107.2 %reduce-scatter.2.cloned.1.call-start = ((), (), s32[]{:S(2)}) async-start(), calls=%async_computation.4 | async-start | bytes 2621440 | tf_op jit(solution)/shard_map/reduce_scatter | solution.py:115
Sparse Core Ops, SparseCore 0:
  9.2 39.4 all-gather.1
  166.1 46.9 reduce-scatter.1

commit v2 on v1

--- a/solution.py
+++ b/solution.py
@@ -10,6 +10,7 @@
 
 BLOCK = 128
 UNROLL = 4
+MESH = pl.DeviceIdType.MESH
 
 
 def attend(unroll, tiles, coef, ids, counts, qt_ref, k_ref, v_ref, num_ref, ml_ref, acc, mx, den):
@@ -89,30 +90,306 @@
     )(ids, counts, query_cols, key_states, value_states)
 
 
+def everyone(sends):
+    barrier = pltpu.get_barrier_semaphore()
+    for device in sends:
+        pl.semaphore_signal(barrier, inc=1, device_id=device, device_id_type=MESH)
+    pl.semaphore_wait(barrier, len(sends))
+
+
+def remote(src, dst, send_sem, recv_sem, device):
+    return pltpu.make_async_remote_copy(
+        src_ref=src,
+        dst_ref=dst,
+        send_sem=send_sem,
+        recv_sem=recv_sem,
+        device_id=device,
+        device_id_type=MESH,
+    )
+
+
+def gather(pairs, q_ref, out_ref, own, own_sem, send_sem, recv_sem, pass_sem, took_sem):
+    own_tiles, heads_here = own.shape[:2]
+    place = lax.axis_index("keys")
+    pair, core = place // 2, place % 2
+    sibling = {"keys": pair * 2 + 1 - core}
+    peers = [{"keys": lax.rem(pair + d, pairs) * 2 + core} for d in range(1, pairs)]
+    for t in range(own_tiles):
+        for h in range(heads_here):
+            tile = q_ref[t * BLOCK : (t + 1) * BLOCK, h * BLOCK : (h + 1) * BLOCK]
+            own[t, h] = tile.T
+    everyone([sibling] + peers)
+    sends, passes = [], []
+    for t in range(own_tiles):
+        for d in range(1, pairs):
+            copy = remote(
+                own.at[t],
+                out_ref.at[pair, core, t],
+                send_sem.at[t, d - 1],
+                recv_sem.at[t, d - 1],
+                peers[d - 1],
+            )
+            copy.start()
+            sends.append((t, d, copy))
+    for t in range(own_tiles):
+        copy = remote(
+            own.at[t],
+            out_ref.at[pair, core, t],
+            pass_sem.at[t, 0],
+            took_sem.at[t, 0],
+            sibling,
+        )
+        copy.start()
+        passes.append(copy)
+    keep = pltpu.make_async_copy(own, out_ref.at[pair, core], own_sem)
+    keep.start()
+    for t, d, copy in sends:
+        copy.wait_recv()
+        source = lax.rem(pair + pairs - d, pairs)
+        block = out_ref.at[source, core, t]
+        onward = remote(block, block, pass_sem.at[t, d], took_sem.at[t, d], sibling)
+        onward.start()
+        passes.append(onward)
+    for t, d, copy in sends:
+        copy.wait_send()
+    keep.wait()
+    for copy in passes:
+        copy.wait()
+
+
+def gather_queries(queries, heads_here, key_groups):
+    own_tiles = queries.shape[0] // BLOCK
+    pairs = key_groups // 2
+    head_dim = queries.shape[1] // heads_here
+    block = (own_tiles, heads_here, head_dim, BLOCK)
+    out = pl.pallas_call(
+        functools.partial(gather, pairs),
+        in_specs=[pl.BlockSpec(memory_space=pltpu.VMEM)],
+        out_specs=pl.BlockSpec(memory_space=pl.ANY),
+        out_shape=jax.ShapeDtypeStruct((pairs, 2) + block, queries.dtype),
+        scratch_shapes=[
+            pltpu.VMEM(block, queries.dtype),
+            pltpu.SemaphoreType.DMA,
+            pltpu.SemaphoreType.DMA((own_tiles, pairs - 1)),
+            pltpu.SemaphoreType.DMA((own_tiles, pairs - 1)),
+            pltpu.SemaphoreType.DMA((own_tiles, pairs)),
+            pltpu.SemaphoreType.DMA((own_tiles, pairs)),
+        ],
+        compiler_params=pltpu.CompilerParams(
+            collective_id=0, has_side_effects=True, vmem_limit_bytes=48 << 20
+        ),
+        name="gather_queries",
+    )(queries)
+    return out.reshape((key_groups * own_tiles,) + block[1:])
+
+
+def merged(parts, coef):
+    best = functools.reduce(jnp.maximum, [ml[0:1] for _, ml in parts])
+    shift = jnp.where(best == -jnp.inf, 0.0, best)
+    factors = [jnp.exp2((ml[0:1] - shift) * coef) for _, ml in parts]
+    num = sum(part.astype(jnp.float32) * f for (part, _), f in zip(parts, factors))
+    den = sum(ml[1:2] * f for (_, ml), f in zip(parts, factors))
+    return num, best, den
+
+
+def finish(
+    pairs,
+    groups,
+    coef,
+    num_ref,
+    ml_ref,
+    w_ref,
+    out_ref,
+    weight,
+    mine,
+    mine_ml,
+    sib,
+    sib_ml,
+    comb,
+    comb_ml,
+    got,
+    got_ml,
+    rows,
+    part,
+    kept,
+    landed,
+    weight_sem,
+    mine_sem,
+    sib_sem,
+    send_sem,
+    recv_sem,
+    z_send,
+    z_recv,
+):
+    own_tiles, heads_here = num_ref.shape[2:4]
+    span = out_ref.shape[1]
+    place, group = lax.axis_index("keys"), lax.axis_index("heads")
+    pair, core = place // 2, place % 2
+    sibling = {"keys": pair * 2 + 1 - core}
+    peers = [{"keys": lax.rem(pair + d, pairs) * 2 + core} for d in range(1, pairs)]
+    others = [{"heads": lax.rem(group + d, groups)} for d in range(1, groups)]
+    load_weight = pltpu.make_async_copy(w_ref, weight, weight_sem)
+    loads = []
+    for t in range(own_tiles):
+        loads.append(
+            (
+                pltpu.make_async_copy(num_ref.at[:, core, t], mine.at[t], mine_sem.at[t, 0]),
+                pltpu.make_async_copy(ml_ref.at[:, core, t], mine_ml.at[t], mine_sem.at[t, 1]),
+            )
+        )
+    everyone([sibling] + peers + others)
+    swaps = []
+    for t in range(own_tiles):
+        swap = (
+            remote(
+                num_ref.at[:, 1 - core, t],
+                sib.at[t],
+                sib_sem.at[0, t, 0],
+                sib_sem.at[1, t, 0],
+                sibling,
+            ),
+            remote(
+                ml_ref.at[:, 1 - core, t],
+                sib_ml.at[t],
+                sib_sem.at[0, t, 1],
+                sib_sem.at[1, t, 1],
+                sibling,
+            ),
+        )
+        for copy in swap + loads[t]:
+            copy.start()
+        swaps.append(swap)
+    load_weight.start()
+
+    sends = []
+    for t in range(own_tiles):
+        for copy in loads[t]:
+            copy.wait()
+        for copy in swaps[t]:
+            copy.wait()
+        here = []
+        for d in list(range(1, pairs)) + [0]:
+            to = lax.rem(pair + d, pairs)
+
+            @pl.loop(0, heads_here)
+            def _(h):
+                num, best, den = merged(
+                    [(mine[t, to, h], mine_ml[t, to, h]), (sib[t, to, h], sib_ml[t, to, h])],
+                    coef,
+                )
+                comb[t, d, h] = num.astype(comb.dtype)
+                comb_ml[t, d, h, 0:1] = best
+                comb_ml[t, d, h, 1:2] = den
+
+            if d:
+                for i, (src, dst) in enumerate([(comb, got), (comb_ml, got_ml)]):
+                    copy = remote(
+                        src.at[t, d],
+                        dst.at[t, d - 1],
+                        send_sem.at[t, d - 1, i],
+                        recv_sem.at[t, d - 1, i],
+                        peers[d - 1],
+                    )
+                    copy.start()
+                    here.append(copy)
+        sends.append(here)
+    load_weight.wait()
+
+    crossing = []
+    for t in range(own_tiles):
+        for copy in sends[t]:
+            copy.wait()
+
+        for h in range(heads_here):
+            parts = [(comb[t, 0, h], comb_ml[t, 0, h])]
+            parts += [(got[t, d, h], got_ml[t, d, h]) for d in range(pairs - 1)]
+            num, _, den = merged(parts, coef)
+            rows[:, h * BLOCK : (h + 1) * BLOCK] = (num / den).T.astype(rows.dtype)
+
+        here = []
+        for d in list(range(1, groups)) + [0]:
+            start = pl.multiple_of(lax.rem(group + d, groups) * span, span)
+            product = jnp.dot(
+                rows[...], weight[:, pl.ds(start, span)], preferred_element_type=jnp.float32
+            )
+            if d:
+                part[t, d - 1] = product.astype(part.dtype)
+                copy = remote(
+                    part.at[t, d - 1],
+                    landed.at[t, d - 1],
+                    z_send.at[t, d - 1],
+                    z_recv.at[t, d - 1],
+                    others[d - 1],
+                )
+                copy.start()
+                here.append(copy)
+            else:
+                kept[t] = product
+        crossing.append(here)
+
+    for t in range(own_tiles):
+        for copy in crossing[t]:
+            copy.wait()
+        total = kept[t]
+        for d in range(groups - 1):
+            total += landed[t, d].astype(jnp.float32)
+        out_ref[t * BLOCK : (t + 1) * BLOCK] = total.astype(out_ref.dtype)
+
+
+def finish_rows(num, ml, out_weight, coef):
+    pairs, _, tiles, heads_here, head_dim, _ = num.shape
+    groups = lax.axis_size("heads")
+    span = out_weight.shape[1] // groups
+    block = (heads_here, head_dim, BLOCK)
+    small = (heads_here, 2, BLOCK)
+    half, full, dma = jnp.bfloat16, jnp.float32, pltpu.SemaphoreType.DMA
+    return pl.pallas_call(
+        functools.partial(finish, pairs, groups, coef),
+        in_specs=[pl.BlockSpec(memory_space=pl.ANY)] * 3,
+        out_specs=pl.BlockSpec(memory_space=pltpu.VMEM),
+        out_shape=jax.ShapeDtypeStruct((tiles * BLOCK, span), half),
+        scratch_shapes=[
+            pltpu.VMEM(out_weight.shape, half),
+            pltpu.VMEM((tiles, pairs) + block, half),
+            pltpu.VMEM((tiles, pairs) + small, full),
+            pltpu.VMEM((tiles, pairs) + block, half),
+            pltpu.VMEM((tiles, pairs) + small, full),
+            pltpu.VMEM((tiles, pairs) + block, half),
+            pltpu.VMEM((tiles, pairs) + small, full),
+            pltpu.VMEM((tiles, pairs - 1) + block, half),
+            pltpu.VMEM((tiles, pairs - 1) + small, full),
+            pltpu.VMEM((BLOCK, heads_here * head_dim), half),
+            pltpu.VMEM((tiles, groups - 1, BLOCK, span), half),
+            pltpu.VMEM((tiles, BLOCK, span), full),
+            pltpu.VMEM((tiles, groups - 1, BLOCK, span), half),
+            dma,
+            dma((tiles, 2)),
+            dma((2, tiles, 2)),
+            dma((tiles, pairs - 1, 2)),
+            dma((tiles, pairs - 1, 2)),
+            dma((tiles, groups - 1)),
+            dma((tiles, groups - 1)),
+        ],
+        compiler_params=pltpu.CompilerParams(
+            collective_id=1, has_side_effects=True, vmem_limit_bytes=56 << 20
+        ),
+        name="merge_and_project",
+    )(num, ml, out_weight)
+
+
 def local(queries, key_states, value_states, block_ids, block_counts, out_weight):
     heads_here, _ = block_ids.shape
     head_dim = key_states.shape[1] // heads_here
-    own_rows = queries.shape[0]
-    own_tiles = own_rows // BLOCK
     key_groups = lax.axis_size("keys")
     coef = head_dim ** (-0.5) * math.log2(math.e)
-    own_cols = queries.reshape(own_tiles, BLOCK, heads_here, head_dim).transpose(0, 2, 3, 1)
-    query_cols = lax.all_gather(own_cols, "keys", axis=0, tiled=True)
+    query_cols = gather_queries(queries, heads_here, key_groups)
     num, ml = partials(
         query_cols, key_states, value_states, block_ids, block_counts[:, 0], coef
     )
-    num = lax.all_to_all(num, "keys", split_axis=0, concat_axis=0, tiled=True)
-    ml = lax.all_to_all(ml, "keys", split_axis=0, concat_axis=0, tiled=True)
-    num = num.reshape(key_groups, own_tiles, heads_here, head_dim, BLOCK)
-    ml = ml.reshape(key_groups, own_tiles, heads_here, 2, BLOCK)
-    best = ml[:, :, :, 0]
-    factor = jnp.exp2((best - best.max(0)) * coef)
-    weight_sum = (ml[:, :, :, 1] * factor).sum(0)
-    row_sum = (num.astype(jnp.float32) * factor[:, :, :, None]).sum(0)
-    attention = (row_sum / weight_sum[:, :, None]).astype(jnp.bfloat16)
-    flat = attention.transpose(0, 3, 1, 2).reshape(own_rows, heads_here * head_dim)
-    part = jnp.dot(flat, out_weight, preferred_element_type=jnp.float32).astype(jnp.bfloat16)
-    return lax.psum_scatter(part, "heads", scatter_dimension=1, tiled=True)
+    shape = (key_groups // 2, 2, queries.shape[0] // BLOCK)
+    num = num.reshape(shape + num.shape[1:])
+    ml = ml.reshape(shape + ml.shape[1:])
+    return finish_rows(num, ml, out_weight, coef)
 
 
 def solution(mesh):

time: 218 us -> 151 us (0.69); the launches traced: 220 us -> 149 us
  waiting for transfers between devices: 136 us -> 0 us
  Pallas kernels: 37.2 us -> 140 us
  between operations: 13.5 us -> 0.05 us
  blocking collectives: 12.2 us -> 0 us
  matrix products: 7.06 us -> 0 us
  starting transfers between devices: 4.58 us -> 0 us
  other arithmetic: 3.6 us -> 0 us
  local copies, waits for them, and re-layouts: 5.99 us -> 8.78 us
    pallas_call x0 -> x2, Pallas kernels: none -> 107 us  [the longest x1 78.1 us: finish_rows(): pl.pallas_call(functools.partial(finish, pairs, groups, coef), in_specs=[...]
    all_to_all x1 -> x0, waiting for transfers between devices: 48.9 us -> none  [local(): num = lax.all_to_all(num, 'keys', split_axis=0, concat_axis=0, tiled=True)]
    reduce_scatter x1 -> x0, waiting for transfers between devices: 47.1 us -> none  [local(): return lax.psum_scatter(part, 'heads', scatter_dimension=1, tiled=True)]
    all_gather x1 -> x0, waiting for transfers between devices: 39.8 us -> none  [local(): query_cols = lax.all_gather(own_cols, 'keys', axis=0, tiled=True)]
    all_to_all x1 -> x0, blocking collectives: 12.2 us -> none  [local(): ml = lax.all_to_all(ml, 'keys', split_axis=0, concat_axis=0, tiled=True)]
    dot_general x1 -> x0, matrix products: 7.06 us -> none  [local(): jnp.dot(flat, out_weight, preferred_element_type=jnp.float32)]
    all_to_all x1 -> x0, starting transfers between devices: 4.53 us -> none  [local(): num = lax.all_to_all(num, 'keys', split_axis=0, concat_axis=0, tiled=True)]
    unnamed x7 -> x13, local copies, waits for them, and re-layouts: 4.43 us -> 8.78 us
  transfers between devices with their start and end apart: 3 -> 0, of which waited for: 3 -> 0; matrix products, arithmetic and copies ran while one was open for 0% -> 0% of each run, Pallas kernels for 0% -> 0%
where the time goes in v2:
time: 151 us; the launch traced here: 149 us
  Pallas kernels  140 us (93%)
  local copies, waits for them, and re-layouts  8.78 us (6%)
    pallas_call x1, Pallas kernels, finish_rows(): pl.pallas_call(functools.partial(finish, pairs, groups, coef), in_specs=[...  78.1 us
    pallas_call x1, Pallas kernels, partials(): pl.pallas_call(functools.partial(attend, UNROLL, tiles, coef), grid_spec=...  33 us
    pallas_call x1, Pallas kernels, gather_queries(): pl.pallas_call(functools.partial(gather, pairs), in_specs=[pl.BlockSpec(m...  29.3 us
    unnamed x13, local copies, waits for them, and re-layouts  8.78 us

profile of v2, /device:TPU:0, one launch (start us, length us, event | category | flops | bytes accessed | tf_op | source)
XLA Modules:
  0.0 149.3 jit_solution(17590517808946677995)
XLA Ops:
  0.0 0.0 copy-start.2
  0.0 1.0 copy-done.2
  1.0 29.3 %gather_queries.1 = bf16[4,2,2,8,128,128]{5,4,3,2,1,0:T(8,128)(2,1)S(1)} custom-call(bf16[256,1024]{1,0:T(8,128)(2,1)S(1)} %copy-done.2), custom_call_target="tpu_custom_call" | custom-call | tf_op jit(solution)/shard_map/gather_queries/pallas_call | solution.py:165
  30.4 0.0 copy-start
  30.4 1.9 %copy-done = bf16[4,2,2,8,128,128]{5,4,3,2,1,0:T(8,128)(2,1)} copy-done((bf16[4,2,2,8,128,128]{5,4,3,2,1,0:T(8,128)(2,1)}, bf16[4,2,2,8,128,128]{5,4,3,2,1,0:T(8,128)(2,1)S(1)}, u32[]{:S(2)}) %copy-start) | copy-done | bytes 4194328
  32.3 0.0 copy-start.4
  32.3 0.7 copy-done.4
  33.0 0.0 copy-start.5
  33.0 0.7 copy-done.5
  33.7 33.0 %block_attention.1 = (bf16[16,8,128,128]{3,2,1,0:T(8,128)(2,1)S(1)}, f32[16,8,2,128]{3,2,1,0:T(2,128)S(1)}) custom-call(s32[8,96]{1,0:T(8,128)S(1)} %copy-done.4, s32[8]{0:T(128)S(1)} %bitcast.7, bf16[16,8,128,128]{3,2,1,0:T(8,128)(2,1)} %bitcast.4, bf16[8192,1024]{1,0:T(8,128)(2,1)} %k_ref.1, bf16[8192,1024]{1,0:T(8,128)(2,1)} %v_ref.1), custom_call_target="tpu_custom_call" | custom-call | tf_op jit(solution)/shard_map/block_attention/pallas_call | solution.py:64
  66.7 0.0 copy-start.1
  66.7 1.9 %copy-done.1 = bf16[16,8,128,128]{3,2,1,0:T(8,128)(2,1)} copy-done((bf16[16,8,128,128]{3,2,1,0:T(8,128)(2,1)}, bf16[16,8,128,128]{3,2,1,0:T(8,128)(2,1)S(1)}, u32[]{:S(2)}) %copy-start.1) | copy-done | bytes 4194328
  68.7 0.0 copy-start.3
  68.7 0.7 copy-done.3
  69.3 78.1 %merge_and_project.1 = bf16[256,1024]{1,0:T(8,128)(2,1)} custom-call(bf16[4,2,2,8,128,128]{5,4,3,2,1,0:T(8,128)(2,1)} %bitcast.5, f32[4,2,2,8,2,128]{5,4,3,2,1,0:T(2,128)} %bitcast.6, bf16[1024,4096]{1,0:T(8,128)(2,1)} %w_ref.1), custom_call_target="tpu_custom_call" | custom-call | tf_op jit(solution)/shard_map/merge_and_project/pallas_call | solution.py:346
  147.4 1.9 %copy.8 = bf16[256,1024]{1,0:T(8,128)(2,1)} copy(bf16[256,1024]{1,0:T(8,128)(2,1)} %merge_and_project.1) | data formatting | bytes 1048576
Async XLA Ops:
  0.0 1.0 copy-start.2
  30.4 1.9 %copy-start = (bf16[4,2,2,8,128,128]{5,4,3,2,1,0:T(8,128)(2,1)}, bf16[4,2,2,8,128,128]{5,4,3,2,1,0:T(8,128)(2,1)S(1)}, u32[]{:S(2)}) copy-start(bf16[4,2,2,8,128,128]{5,4,3,2,1,0:T(8,128)(2,1)S(1)} %gather_queries.1) | copy-start | bytes 12582916
  32.3 0.7 copy-start.4
  33.0 0.7 copy-start.5
  66.7 1.9 %copy-start.1 = (bf16[16,8,128,128]{3,2,1,0:T(8,128)(2,1)}, bf16[16,8,128,128]{3,2,1,0:T(8,128)(2,1)S(1)}, u32[]{:S(2)}) copy-start(bf16[16,8,128,128]{3,2,1,0:T(8,128)(2,1)S(1)} %get-tuple-element.7) | copy-start | bytes 12582916
  68.7 0.7 copy-start.3

commit v3 on v2

--- a/solution.py
+++ b/solution.py
@@ -9,12 +9,13 @@
 from jax.sharding import PartitionSpec as P
 
 BLOCK = 128
-UNROLL = 4
+UNROLL = 8
+VMEM_BYTES = 60 << 20
 MESH = pl.DeviceIdType.MESH
 
 
-def attend(unroll, tiles, coef, ids, counts, qt_ref, k_ref, v_ref, num_ref, ml_ref, acc, mx, den):
-    head = pl.program_id(0)
+def attend(unroll, tiles, coef, first, ids, counts, qt_ref, k_ref, v_ref, num_ref, ml_ref, acc, mx, den):
+    head = first + pl.program_id(0)
     query_tiles = qt_ref.shape[0]
     count = counts[head]
     acc[...] = jnp.zeros_like(acc)
@@ -57,19 +58,19 @@
     ml_ref[:, 0, 1:2] = den[:query_tiles]
 
 
-def partials(query_cols, key_states, value_states, ids, counts, coef):
+def partials(query_cols, key_states, value_states, ids, counts, coef, first):
     query_tiles, heads_here, head_dim, _ = query_cols.shape
     key_rows = key_states.shape[0]
     tiles = key_rows // BLOCK
     return pl.pallas_call(
-        functools.partial(attend, UNROLL, tiles, coef),
+        functools.partial(attend, UNROLL, tiles, coef, first),
         grid_spec=pltpu.PrefetchScalarGridSpec(
             num_scalar_prefetch=2,
             grid=(heads_here,),
             in_specs=[
                 pl.BlockSpec((query_tiles, 1, head_dim, BLOCK), lambda h, *_: (0, h, 0, 0)),
-                pl.BlockSpec((key_rows, head_dim), lambda h, *_: (0, h)),
-                pl.BlockSpec((key_rows, head_dim), lambda h, *_: (0, h)),
+                pl.BlockSpec((key_rows, head_dim), lambda h, *_: (0, first + h)),
+                pl.BlockSpec((key_rows, head_dim), lambda h, *_: (0, first + h)),
             ],
             out_specs=[
                 pl.BlockSpec((query_tiles, 1, head_dim, BLOCK), lambda h, *_: (0, h, 0, 0)),
@@ -85,7 +86,12 @@
             jax.ShapeDtypeStruct((query_tiles, heads_here, head_dim, BLOCK), jnp.bfloat16),
             jax.ShapeDtypeStruct((query_tiles, heads_here, 2, BLOCK), jnp.float32),
         ],
-        compiler_params=pltpu.CompilerParams(vmem_limit_bytes=48 << 20),
+        compiler_params=pltpu.CompilerParams(vmem_limit_bytes=VMEM_BYTES),
+        cost_estimate=pl.CostEstimate(
+            flops=heads_here * ids.shape[1] * 4 * BLOCK**3,
+            bytes_accessed=heads_here * key_rows * head_dim * 4,
+            transcendentals=heads_here * ids.shape[1] * BLOCK**2,
+        ),
         name="block_attention",
     )(ids, counts, query_cols, key_states, value_states)
 
@@ -108,8 +114,9 @@
     )
 
 
-def gather(pairs, q_ref, out_ref, own, own_sem, send_sem, recv_sem, pass_sem, took_sem):
+def gather(pairs, q_ref, out_ref, rest_ref, own, own_sem, send_sem, recv_sem, pass_sem, took_sem):
     own_tiles, heads_here = own.shape[:2]
+    later_heads = rest_ref.shape[1]
     place = lax.axis_index("keys")
     pair, core = place // 2, place % 2
     sibling = {"keys": pair * 2 + 1 - core}
@@ -143,6 +150,10 @@
         passes.append(copy)
     keep = pltpu.make_async_copy(own, out_ref.at[pair, core], own_sem)
     keep.start()
+    for t in range(own_tiles):
+        for h in range(later_heads):
+            at = (heads_here + h) * BLOCK
+            rest_ref[t, h] = q_ref[t * BLOCK : (t + 1) * BLOCK, at : at + BLOCK].T
     for t, d, copy in sends:
         copy.wait_recv()
         source = lax.rem(pair + pairs - d, pairs)
@@ -157,16 +168,20 @@
         copy.wait()
 
 
-def gather_queries(queries, heads_here, key_groups):
+def gather_queries(queries, heads_here, first_heads, key_groups):
     own_tiles = queries.shape[0] // BLOCK
     pairs = key_groups // 2
     head_dim = queries.shape[1] // heads_here
-    block = (own_tiles, heads_here, head_dim, BLOCK)
-    out = pl.pallas_call(
+    block = (own_tiles, first_heads, head_dim, BLOCK)
+    rest = (own_tiles, heads_here - first_heads, head_dim, BLOCK)
+    out, later = pl.pallas_call(
         functools.partial(gather, pairs),
         in_specs=[pl.BlockSpec(memory_space=pltpu.VMEM)],
-        out_specs=pl.BlockSpec(memory_space=pl.ANY),
-        out_shape=jax.ShapeDtypeStruct((pairs, 2) + block, queries.dtype),
+        out_specs=[pl.BlockSpec(memory_space=pl.ANY), pl.BlockSpec(memory_space=pltpu.VMEM)],
+        out_shape=[
+            jax.ShapeDtypeStruct((pairs, 2) + block, queries.dtype),
+            jax.ShapeDtypeStruct(rest, queries.dtype),
+        ],
         scratch_shapes=[
             pltpu.VMEM(block, queries.dtype),
             pltpu.SemaphoreType.DMA,
@@ -176,11 +191,12 @@
             pltpu.SemaphoreType.DMA((own_tiles, pairs)),
         ],
         compiler_params=pltpu.CompilerParams(
-            collective_id=0, has_side_effects=True, vmem_limit_bytes=48 << 20
+            collective_id=0, has_side_effects=True, vmem_limit_bytes=VMEM_BYTES
         ),
         name="gather_queries",
     )(queries)
-    return out.reshape((key_groups * own_tiles,) + block[1:])
+    later = lax.all_gather(later, "keys", axis=0, tiled=True)
+    return out.reshape((key_groups * own_tiles,) + block[1:]), later
 
 
 def merged(parts, coef):
@@ -196,8 +212,8 @@
     pairs,
     groups,
     coef,
-    num_ref,
-    ml_ref,
+    num_refs,
+    ml_refs,
     w_ref,
     out_ref,
     weight,
@@ -221,7 +237,8 @@
     z_send,
     z_recv,
 ):
-    own_tiles, heads_here = num_ref.shape[2:4]
+    own_tiles = mine.shape[0]
+    heads_here = mine.shape[2]
     span = out_ref.shape[1]
     place, group = lax.axis_index("keys"), lax.axis_index("heads")
     pair, core = place // 2, place % 2
@@ -229,35 +246,33 @@
     peers = [{"keys": lax.rem(pair + d, pairs) * 2 + core} for d in range(1, pairs)]
     others = [{"heads": lax.rem(group + d, groups)} for d in range(1, groups)]
     load_weight = pltpu.make_async_copy(w_ref, weight, weight_sem)
-    loads = []
-    for t in range(own_tiles):
-        loads.append(
-            (
-                pltpu.make_async_copy(num_ref.at[:, core, t], mine.at[t], mine_sem.at[t, 0]),
-                pltpu.make_async_copy(ml_ref.at[:, core, t], mine_ml.at[t], mine_sem.at[t, 1]),
-            )
-        )
+    sources, at = [], 0
+    for num_ref, ml_ref in zip(num_refs, ml_refs):
+        part_heads = pl.ds(at, num_ref.shape[3])
+        sources += [(num_ref, mine, sib, part_heads), (ml_ref, mine_ml, sib_ml, part_heads)]
+        at += num_ref.shape[3]
     everyone([sibling] + peers + others)
-    swaps = []
-    for t in range(own_tiles):
-        swap = (
-            remote(
-                num_ref.at[:, 1 - core, t],
-                sib.at[t],
-                sib_sem.at[0, t, 0],
-                sib_sem.at[1, t, 0],
-                sibling,
-            ),
-            remote(
-                ml_ref.at[:, 1 - core, t],
-                sib_ml.at[t],
-                sib_sem.at[0, t, 1],
-                sib_sem.at[1, t, 1],
-                sibling,
-            ),
-        )
-        for copy in swap + loads[t]:
+    loads, swaps = [], []
+    for t in range(own_tiles):
+        load, swap = [], []
+        for i, (src, dst, far, part_heads) in enumerate(sources):
+            swap.append(
+                remote(
+                    src.at[:, 1 - core, t],
+                    far.at[t, :, part_heads],
+                    sib_sem.at[0, t, i],
+                    sib_sem.at[1, t, i],
+                    sibling,
+                )
+            )
+            load.append(
+                pltpu.make_async_copy(
+                    src.at[:, core, t], dst.at[t, :, part_heads], mine_sem.at[t, i]
+                )
+            )
+        for copy in swap + load:
             copy.start()
+        loads.append(load)
         swaps.append(swap)
     load_weight.start()
 
@@ -295,7 +310,25 @@
         sends.append(here)
     load_weight.wait()
 
-    crossing = []
+    def hops(t, shard):
+        found = []
+        for way, step in enumerate((1, groups - 1)):
+            copy = remote(
+                part.at[way, t, shard],
+                landed.at[way, t, shard],
+                z_send.at[way, t, shard],
+                z_recv.at[way, t, shard],
+                {"heads": lax.rem(group + step, groups)},
+            )
+            if way == 0:
+                found.append((group < shard, group > 0, copy))
+            else:
+                found.append((group > shard, group < groups - 1, copy))
+        return found
+
+    order = []
+    for shard in range((groups + 1) // 2):
+        order += [groups - 1 - shard] + [shard] * (shard != groups - 1 - shard)
     for t in range(own_tiles):
         for copy in sends[t]:
             copy.wait()
@@ -306,46 +339,64 @@
             num, _, den = merged(parts, coef)
             rows[:, h * BLOCK : (h + 1) * BLOCK] = (num / den).T.astype(rows.dtype)
 
-        here = []
-        for d in list(range(1, groups)) + [0]:
-            start = pl.multiple_of(lax.rem(group + d, groups) * span, span)
-            product = jnp.dot(
-                rows[...], weight[:, pl.ds(start, span)], preferred_element_type=jnp.float32
-            )
-            if d:
-                part[t, d - 1] = product.astype(part.dtype)
-                copy = remote(
-                    part.at[t, d - 1],
-                    landed.at[t, d - 1],
-                    z_send.at[t, d - 1],
-                    z_recv.at[t, d - 1],
-                    others[d - 1],
-                )
-                copy.start()
-                here.append(copy)
-            else:
-                kept[t] = product
-        crossing.append(here)
-
-    for t in range(own_tiles):
-        for copy in crossing[t]:
-            copy.wait()
-        total = kept[t]
-        for d in range(groups - 1):
-            total += landed[t, d].astype(jnp.float32)
-        out_ref[t * BLOCK : (t + 1) * BLOCK] = total.astype(out_ref.dtype)
-
-
-def finish_rows(num, ml, out_weight, coef):
-    pairs, _, tiles, heads_here, head_dim, _ = num.shape
+        for shard in order:
+            kept[t, shard] = jnp.dot(
+                rows[...],
+                weight[:, shard * span : (shard + 1) * span],
+                preferred_element_type=jnp.float32,
+            )
+            for way, hop in enumerate(hops(t, shard)):
+                passing, inner, copy = hop
+
+                @pl.when(passing)
+                def _():
+                    @pl.when(inner)
+                    def _():
+                        copy.wait_recv()
+                        part[way, t, shard] = (
+                            kept[t, shard] + landed[way, t, shard].astype(jnp.float32)
+                        ).astype(part.dtype)
+
+                    @pl.when(jnp.logical_not(inner))
+                    def _():
+                        part[way, t, shard] = kept[t, shard].astype(part.dtype)
+
+                    copy.start()
+
+    for t in range(own_tiles):
+        for shard in range(groups):
+
+            @pl.when(group == shard)
+            def _():
+                here = pl.ds(t * BLOCK, BLOCK)
+                total = kept[t, shard]
+                for way, (_, _, copy) in enumerate(hops(t, shard)):
+                    if (shard > 0) if way == 0 else (shard < groups - 1):
+                        copy.wait_recv()
+                        total += landed[way, t, shard].astype(jnp.float32)
+                out_ref[here] = total.astype(out_ref.dtype)
+
+    for t in range(own_tiles):
+        for shard in range(groups):
+            for passing, _, copy in hops(t, shard):
+
+                @pl.when(passing)
+                def _():
+                    copy.wait_send()
+
+
+def finish_rows(nums, mls, out_weight, coef):
+    pairs, _, tiles, _, head_dim, _ = nums[0].shape
+    heads_here = sum(num.shape[3] for num in nums)
     groups = lax.axis_size("heads")
     span = out_weight.shape[1] // groups
     block = (heads_here, head_dim, BLOCK)
     small = (heads_here, 2, BLOCK)
+    anywhere = pl.BlockSpec(memory_space=pl.ANY)
     half, full, dma = jnp.bfloat16, jnp.float32, pltpu.SemaphoreType.DMA
     return pl.pallas_call(
         functools.partial(finish, pairs, groups, coef),
-        in_specs=[pl.BlockSpec(memory_space=pl.ANY)] * 3,
+        in_specs=[[anywhere] * len(nums), [anywhere] * len(mls), anywhere],
         out_specs=pl.BlockSpec(memory_space=pltpu.VMEM),
         out_shape=jax.ShapeDtypeStruct((tiles * BLOCK, span), half),
         scratch_shapes=[
@@ -359,22 +410,22 @@
             pltpu.VMEM((tiles, pairs - 1) + block, half),
             pltpu.VMEM((tiles, pairs - 1) + small, full),
             pltpu.VMEM((BLOCK, heads_here * head_dim), half),
-            pltpu.VMEM((tiles, groups - 1, BLOCK, span), half),
-            pltpu.VMEM((tiles, BLOCK, span), full),
-            pltpu.VMEM((tiles, groups - 1, BLOCK, span), half),
+            pltpu.VMEM((2, tiles, groups, BLOCK, span), half),
+            pltpu.VMEM((tiles, groups, BLOCK, span), full),
+            pltpu.VMEM((2, tiles, groups, BLOCK, span), half),
             dma,
-            dma((tiles, 2)),
-            dma((2, tiles, 2)),
+            dma((tiles, 2 * len(nums))),
+            dma((2, tiles, 2 * len(nums))),
             dma((tiles, pairs - 1, 2)),
             dma((tiles, pairs - 1, 2)),
-            dma((tiles, groups - 1)),
-            dma((tiles, groups - 1)),
+            dma((2, tiles, groups)),
+            dma((2, tiles, groups)),
         ],
         compiler_params=pltpu.CompilerParams(
-            collective_id=1, has_side_effects=True, vmem_limit_bytes=56 << 20
+            collective_id=1, has_side_effects=True, vmem_limit_bytes=VMEM_BYTES
         ),
         name="merge_and_project",
-    )(num, ml, out_weight)
+    )(nums, mls, out_weight)
 
 
 def local(queries, key_states, value_states, block_ids, block_counts, out_weight):
@@ -382,14 +433,17 @@
     head_dim = key_states.shape[1] // heads_here
     key_groups = lax.axis_size("keys")
     coef = head_dim ** (-0.5) * math.log2(math.e)
-    query_cols = gather_queries(queries, heads_here, key_groups)
-    num, ml = partials(
-        query_cols, key_states, value_states, block_ids, block_counts[:, 0], coef
-    )
+    first_heads = heads_here // 2
+    gathered = gather_queries(queries, heads_here, first_heads, key_groups)
     shape = (key_groups // 2, 2, queries.shape[0] // BLOCK)
-    num = num.reshape(shape + num.shape[1:])
-    ml = ml.reshape(shape + ml.shape[1:])
-    return finish_rows(num, ml, out_weight, coef)
+    nums, mls = [], []
+    for first, query_cols in zip((0, first_heads), gathered):
+        num, ml = partials(
+            query_cols, key_states, value_states, block_ids, block_counts[:, 0], coef, first
+        )
+        nums.append(num.reshape(shape + num.shape[1:]))
+        mls.append(ml.reshape(shape + ml.shape[1:]))
+    return finish_rows(nums, mls, out_weight, coef)
 
 
 def solution(mesh):

time: 151 us -> 149 us (0.987)
  Pallas kernels: 140 us -> 119 us
  between operations: 0.05 us -> 13.4 us
  waiting for transfers between devices: 0 us -> 12.9 us
  local copies, waits for them, and re-layouts: 8.78 us -> 1.87 us
    all_gather x0 -> x1, waiting for transfers between devices: none -> 12.9 us  [gather_queries(): later = lax.all_gather(later, 'keys', axis=0, tiled=True)]
    pallas_call x1, Pallas kernels: 29.3 us -> 19.8 us  [gather_queries(): pl.pallas_call(functools.partial(gather, pairs), in_specs=[pl.BlockSpec(m...]
    pallas_call x1, Pallas kernels: 78.1 us -> 68.7 us  [finish_rows(): pl.pallas_call(functools.partial(finish, pairs, groups, coef), in_specs=[...]
    unnamed x13 -> x1, local copies, waits for them, and re-layouts: 8.78 us -> 1.87 us
    pallas_call x1 -> x2, Pallas kernels: 33 us -> 30.6 us  [partials(): pl.pallas_call(functools.partial(attend, UNROLL, tiles, coef, first), gri...]
  transfers between devices with their start and end apart: 0 -> 1, of which waited for: 0 -> 1; matrix products, arithmetic and copies ran while one was open for 0% -> 0% of each run, Pallas kernels for 0% -> 11%
where the time goes in v3:
time: 149 us; the launch traced here: 147 us
  Pallas kernels  119 us (80%)
  between operations  13.4 us (9%)
  waiting for transfers between devices  12.9 us (9%)
  local copies, waits for them, and re-layouts  1.87 us (1%)
    pallas_call x1, Pallas kernels, finish_rows(): pl.pallas_call(functools.partial(finish, pairs, groups, coef), in_specs=[...  68.7 us
    pallas_call x2, Pallas kernels, partials(): pl.pallas_call(functools.partial(attend, UNROLL, tiles, coef, first), gri...  30.6 us
    pallas_call x1, Pallas kernels, gather_queries(): pl.pallas_call(functools.partial(gather, pairs), in_specs=[pl.BlockSpec(m...  19.8 us
    all_gather x1, waiting for transfers between devices, gather_queries(): later = lax.all_gather(later, 'keys', axis=0, tiled=True)  12.9 us
  transfers between devices with their start and end apart: 1, of which 1 were waited for; matrix products, arithmetic and copies ran while one was open for 0% of the time, Pallas kernels for 11%

profile of v3, /device:TPU:0, one launch (start us, length us, event | category | flops | bytes accessed | tf_op | source)
XLA Modules:
  0.0 147.4 jit_solution(2872520384698985801)
XLA Ops:
  6.5 0.0 all-gather.2.cloned.1.call-start
  6.5 19.8 %gather_queries.1 = (bf16[4,2,2,4,128,128]{5,4,3,2,1,0:T(8,128)(2,1)}, bf16[2,4,128,128]{3,2,1,0:T(8,128)(2,1)}) custom-call(bf16[256,1024]{1,0:T(8,128)(2,1)} %q_ref.1), custom_call_target="tpu_custom_call" | custom-call | tf_op jit(solution)/shard_map/gather_queries/pallas_call | solution.py:177
  26.4 0.0 all-gather.2.cloned.1.call-update
  26.4 16.2 %block_attention.2 = (bf16[16,4,128,128]{3,2,1,0:T(8,128)(2,1)}, f32[16,4,2,128]{3,2,1,0:T(2,128)}) custom-call(s32[8,96]{1,0:T(8,128)} %ids.3, s32[8]{0:T(128)} %bitcast.11, bf16[16,4,128,128]{3,2,1,0:T(8,128)(2,1)} %bitcast.6, bf16[8192,1024]{1,0:T(8,128)(2,1)} %k_ref.3, bf16[8192,1024]{1,0:T(8,128)(2,1)} %v_ref.3), custom_call_target="tpu_custom_call" | custom-call | flops 3221225472 | bytes 16777216 | tf_op jit(solution)/shard_map/block_attention/pallas_call | solution.py:65
  42.5 12.9 %all-gather.2.cloned.1.call-done.qt_ref = bf16[16,4,128,128]{3,2,1,0:T(8,128)(2,1)} async-done(((bf16[2,4,128,128]{3,2,1,0:T(8,128)(2,1)}), bf16[16,4,128,128]{3,2,1,0:T(8,128)(2,1)}) %all-gather.2.cloned.1.call-update) | async-done | bytes 2097168 | tf_op jit(solution)/shard_map/all_gather | solution.py:198
  55.5 14.5 %block_attention.3 = (bf16[16,4,128,128]{3,2,1,0:T(8,128)(2,1)}, f32[16,4,2,128]{3,2,1,0:T(2,128)}) custom-call(s32[8,96]{1,0:T(8,128)} %ids.3, s32[8]{0:T(128)} %bitcast.12, bf16[16,4,128,128]{3,2,1,0:T(8,128)(2,1)} %all-gather.2.cloned.1.call-done.qt_ref, bf16[8192,1024]{1,0:T(8,128)(2,1)} %k_ref.3, bf16[8192,1024]{1,0:T(8,128)(2,1)} %v_ref.3), custom_call_target="tpu_custom_call" | custom-call | flops 3221225472 | bytes 16777216 | tf_op jit(solution)/shard_map/block_attention/pallas_call | solution.py:65
  69.9 68.7 %merge_and_project.1 = bf16[256,1024]{1,0:T(8,128)(2,1)} custom-call(bf16[4,2,2,4,128,128]{5,4,3,2,1,0:T(8,128)(2,1)} %bitcast.7, bf16[4,2,2,4,128,128]{5,4,3,2,1,0:T(8,128)(2,1)} %bitcast.8, f32[4,2,2,4,2,128]{5,4,3,2,1,0:T(2,128)} %bitcast.9, f32[4,2,2,4,2,128]{5,4,3,2,1,0:T(2,128)} %bitcast.10, bf16[1024,4096]{1,0:T(8,128)(2,1)} %w_ref.1), custom_call_target="tpu_custom_call" | custom-call | tf_op jit(solution)/shard_map/merge_and_project/pallas_call | solution.py:397
  138.6 1.9 %copy.8 = bf16[256,1024]{1,0:T(8,128)(2,1)} copy(bf16[256,1024]{1,0:T(8,128)(2,1)} %merge_and_project.1) | data formatting | bytes 1048576
Async XLA Ops:
  6.5 48.9 %all-gather.2.cloned.1.call-start = ((), (), s32[]{:S(2)}) async-start(), calls=%async_computation | async-start | bytes 2359296 | tf_op jit(solution)/shard_map/all_gather | solution.py:198
Sparse Core Ops, SparseCore 0:
  26.5 28.9 all-gather.1
